TPU v7x, 32 devices: a whole 2x2x4 slice. The times are simulated.
32 devices in a mesh: section: 8 (over z, y), dp: 4 (over x, core).
Axes of the slice: x: 2, y: 2, z: 4, core: 2. Of those that a mesh axis runs over, the one named last changes fastest.
Arguments:
- saved_input: bfloat16 [8, 512, 12288], P('section', 'dp'), may hold values from -6 to 6
- norm_gain: float32 [8, 12288], P('section'), may hold values from 0.25 to 1.75
- left_in: bfloat16 [8, 512, 64], P('section', 'dp'), may hold values from -6 to 6
- right_in: bfloat16 [8, 12288, 64], P('section', 'dp'), may hold values from -0.75 to 0.75
- basis: bfloat16 [8, 12288, 64], P('section', 'dp'), may hold values from -0.0546875 to 0.0546875
Outputs:
- gain_grad: float32 [8, 12288], P('section', 'dp')
- bias_grad: float32 [8, 12288], P('section', 'dp')
- left_out: bfloat16 [8, 512, 64], P('section', 'dp')
- right_out: bfloat16 [8, 12288, 64], P('section', 'dp')
All inputs are finite; a program needn't handle non-finite values.
Results may differ from a plain program's by a relative error of at most 0.02.
Values may be sent and summed in bfloat16 or wider, within the bound.
A program may use at most 64 MiB of HBM per device.

v0:
```python
import jax
import jax.numpy as jnp
from jax import lax
from jax.sharding import PartitionSpec as P


def shifted(x, axis, by):
    size = lax.axis_size(axis)
    pairs = [(i, i + by) for i in range(size) if 0 <= i + by < size]
    return lax.ppermute(x, axis, pairs)


def replica_sums(terms):
    totals = lax.psum(terms.astype(jnp.bfloat16), "dp").astype(jnp.float32)
    width = terms.shape[1] // lax.axis_size("dp")
    return lax.dynamic_slice_in_dim(totals, lax.axis_index("dp") * width, width, 1)


def on_device(saved_input, norm_gain, left_in, right_in, basis):
    left = left_in[0]
    rebuilt = jnp.dot(
        left,
        lax.all_gather(right_in, "dp", axis=1, tiled=True)[0].T,
        preferred_element_type=jnp.float32,
    )
    values = saved_input[0].astype(jnp.float32)
    center = values - jnp.mean(values, axis=1, keepdims=True)
    inverse = lax.rsqrt(jnp.mean(center * center, axis=1, keepdims=True) + 1e-05)
    normed = center * inverse
    tokens_all = saved_input.shape[1] * lax.axis_size("dp")
    factor = 1.0 / jnp.sqrt(jnp.float32(tokens_all))
    terms = jnp.stack([jnp.sum(rebuilt * normed, axis=0), jnp.sum(rebuilt, axis=0)]) * factor
    scaled = rebuilt * norm_gain[0][None, :]
    first = jnp.mean(scaled, axis=1, keepdims=True)
    second = jnp.mean(scaled * normed, axis=1, keepdims=True)
    boundary = (inverse * (scaled - first - normed * second)).astype(jnp.bfloat16)
    columns = boundary
    power = jnp.dot(
        columns,
        lax.all_gather(basis, "dp", axis=1, tiled=True)[0],
        preferred_element_type=jnp.float32,
    )
    gram_local = jnp.dot(power.T, power, precision=lax.Precision.HIGHEST)
    gram = lax.psum(gram_local, "dp")
    lower = jnp.linalg.cholesky(gram)
    ortho = jax.scipy.linalg.solve_triangular(lower, power.T, lower=True).T.astype(jnp.bfloat16)
    columns = boundary
    feature_share = lax.psum_scatter(
        jnp.dot(columns.T, ortho, preferred_element_type=jnp.float32).astype(jnp.bfloat16),
        "dp",
        scatter_dimension=0,
        tiled=True,
    )
    shares = replica_sums(terms)
    moved_left, moved_right = shifted((ortho, feature_share), "section", -1)
    return (shares[0][None], shares[1][None], moved_left[None], moved_right[None])


def solution(mesh):
    placed = (
        P("section", "dp", None),
        P("section", None),
        P("section", "dp", None),
        P("section", "dp", None),
        P("section", "dp", None),
    )
    return jax.shard_map(
        on_device,
        mesh=mesh,
        in_specs=placed,
        out_specs=(
            P("section", "dp"),
            P("section", "dp"),
            P("section", "dp", None),
            P("section", "dp", None),
        ),
        check_vma=False,
    )
```

profile of v0, /device:TPU:0, one launch (start us, length us, event | category | flops | bytes accessed | tf_op | source)
XLA Modules:
  0.0 131.8 jit_solution(7949773698687340338)
XLA Ops:
  7.2 0.0 copy-start
  7.2 0.0 all-gather.3.cloned.1.call-start
  7.2 0.7 all-gather.3.cloned.1.call-update
  7.9 0.0 all-gather.5.cloned.1.call-start
  8.0 0.7 all-gather.5.cloned.1.call-update
  8.7 0.0 reduce-scatter.2.cloned.1.call-start
  8.7 2.4 %convert_reduce_fusion = f32[128]{0:T(128)S(1)} fusion(bf16[1,128,12288]{2,1,0:T(8,128)(2,1)} %param.5), kind=kLoop, calls=%fused_computation.1 | loop fusion | flops 3145600 | bytes 3146240 | tf_op jit(solution)/shard_map/reduce_sum | solution.py:27
  11.1 2.9 %fusion.11 = f32[128]{0:T(128)S(1)} fusion(bf16[1,128,12288]{2,1,0:T(8,128)(2,1)} %param.5, f32[128]{0:T(128)S(1)} %broadcast_multiply_fusion.2), kind=kLoop, calls=%fused_computation.14 | loop fusion | flops 6291328 | bytes 3146752 | tf_op jit(solution)/shard_map/reduce_sum | solution.py:28
  14.0 18.0 %all-gather.3.cloned.1.call-done = bf16[1,12288,64]{1,2,0:T(8,128)(2,1)} async-done(((bf16[1,3072,64]{1,2,0:T(8,128)(2,1)}), bf16[1,12288,64]{1,2,0:T(8,128)(2,1)}) %all-gather.3.cloned.1.call-update) | async-done | bytes 1572880 | tf_op jit(solution)/shard_map/all_gather | solution.py:23
  32.0 4.1 %fusion.7 = (f32[128]{0:T(128)S(1)}, f32[12288]{0:T(1024)S(1)}, f32[128]{0:T(128)S(1)}, f32[12288]{0:T(1024)S(1)}, f32[128,12288]{1,0:T(8,128)S(1)}) fusion(bf16[1,128,12288]{2,1,0:T(8,128)(2,1)S(1)} %copy-done.1, f32[12288]{0:T(1024)S(1)} %bitcast.60, f32[128]{0:T(128)S(1)} %add_rsqrt_fusion, f32[128]{0:T(128)S(1)} %broadcast_multiply_fusion.2, ...), kind=kOutput, calls=%fused_computation.10 | convolution fusion | flops 217030400 | bytes 11175936 | tf_op jit(solution)/shard_map/dot_general | solution.py:21
  36.2 3.0 %fusion.10 = bf16[128,12288]{1,0:T(8,128)(2,1)} fusion(bf16[1,128,12288]{2,1,0:T(8,128)(2,1)S(1)} %copy-done.1, f32[128,12288]{1,0:T(8,128)S(1)} %get-tuple-element.10, f32[128]{0:T(128)S(1)} %get-tuple-element.11, f32[128]{0:T(128)S(1)} %get-tuple-element.12, f32[12288]{0:T(1024)S(1)} %bitcast.61, f32[128]{0:T(128)S(1)} %add_rsqrt_fusion, ...), kind=kLoop, calls=%fused_computation.13 | loop fusion | flops 14155776 | bytes 12634112 | tf_op jit(solution)/shard_map/convert_element_type | solution.py:36
  39.2 14.0 %all-gather.5.cloned.1.call-done = bf16[1,12288,64]{1,2,0:T(8,128)(2,1)} async-done(((bf16[1,3072,64]{1,2,0:T(8,128)(2,1)}), bf16[1,12288,64]{1,2,0:T(8,128)(2,1)}) %all-gather.5.cloned.1.call-update) | async-done | bytes 1572880 | tf_op jit(solution)/shard_map/all_gather | solution.py:40
  53.2 3.6 %fusion.12 = f32[128,64]{0,1:T(8,128)S(1)} fusion(bf16[128,12288]{1,0:T(8,128)(2,1)} %fusion.10, bf16[1,12288,64]{1,2,0:T(8,128)(2,1)} %all-gather.5.cloned.1.call-done), kind=kOutput, calls=%fused_computation.16 | convolution fusion | flops 201326592 | bytes 4751360 | tf_op jit(solution)/shard_map/dot_general | solution.py:38
  56.8 0.2 fusion.22
  57.0 10.4 %psum.15 = f32[64,64]{0,1:T(8,128)S(1)} all-reduce(f32[64,64]{0,1:T(8,128)S(1)} %fusion.22), channel_id=1, replica_groups=mesh['section'=8,'dp'=4] {'dp'}, use_global_device_ids=true, to_apply=%region_7.8 | all-reduce | flops 4096 | bytes 32768 | tf_op jit(solution)/shard_map/psum | solution.py:44
  67.4 0.1 copy.10
  67.5 5.8 %cholesky.16 = f32[64,64]{1,0:T(8,128)S(1)} custom-call(f32[64,64]{1,0:T(8,128)S(1)} %fusion.19), custom_call_target="Cholesky" | custom-call | tf_op jit(solution)/shard_map/jit(cholesky)/cholesky | solution.py:45
  73.4 0.6 compare_reduce_fusion
  74.0 0.7 fusion.17
  74.7 4.9 %custom-call.7 = f32[1,64,64]{1,2,0:T(8,128)S(1)} custom-call(f32[1,64,64]{2,1,0:T(8,128)S(1)} %fusion.17), custom_call_target="InvertDiagBlocksLowerTriangular" | custom-call | tf_op jit(solution)/shard_map/jit(_solve_triangular)/triangular_solve | solution.py:46
  79.6 0.3 convolution_convert_fusion.1
  79.8 1.7 %convolution_convert_fusion = bf16[12288,64]{0,1:T(8,128)(2,1)} fusion(bf16[128,64]{0,1:T(8,128)(2,1)S(1)} %convolution_convert_fusion.1, bf16[128,12288]{1,0:T(8,128)(2,1)S(1)} %copy-done.2), kind=kOutput, calls=%fused_computation | convolution fusion | flops 202113024 | bytes 4734976 | tf_op jit(solution)/shard_map/dot_general | solution.py:49
  81.6 0.0 reduce-scatter.2.cloned.1.call-update
  81.6 1.3 collective-permute-start
  82.9 0.1 fusion.16
  83.0 10.6 %psum.14 = bf16[2,12288]{1,0:T(2,128)(2,1)S(1)} all-reduce(bf16[2,12288]{1,0:T(2,128)(2,1)S(1)} %fusion.16), channel_id=1, replica_groups=mesh['section'=8,'dp'=4] {'dp'}, use_global_device_ids=true, to_apply=%region_4.0 | all-reduce | flops 24576 | bytes 98304 | tf_op jit(solution)/shard_map/psum | solution.py:14
  93.6 17.4 %reduce-scatter.2.cloned.1.call-done = bf16[3072,64]{0,1:T(8,128)(2,1)} async-done(((bf16[12288,64]{0,1:T(8,128)(2,1)}), bf16[3072,64]{0,1:T(8,128)(2,1)}) %reduce-scatter.2.cloned.1.call-update) | async-done | bytes 393232 | tf_op jit(solution)/shard_map/reduce_scatter | solution.py:48
  111.0 1.3 collective-permute-start.1
  112.3 0.6 fusion.21
  112.9 11.0 %collective-permute-done.1 = bf16[3072,64]{0,1:T(8,128)(2,1)S(1)} collective-permute-done((bf16[3072,64]{0,1:T(8,128)(2,1)}, bf16[3072,64]{0,1:T(8,128)(2,1)S(1)}, u32[]{:S(2)}, u32[]{:S(2)}) %collective-permute-start.1) | collective-permute-done | bytes 393248 | tf_op jit(solution)/shard_map/ppermute | solution.py:10
  124.0 0.6 copy.14
  124.6 0.7 copy.15
  (14 shorter events, 0.1 us)
Async XLA Ops:
  7.2 24.8 %copy-start = (bf16[1,128,64]{1,2,0:T(8,128)(2,1)S(1)}, bf16[1,128,64]{1,2,0:T(8,128)(2,1)}, u32[]{:S(2)}) copy-start(bf16[1,128,64]{1,2,0:T(8,128)(2,1)} %param.7) | copy-start | bytes 49156
  7.2 24.8 %copy-start.1 = (bf16[1,128,12288]{2,1,0:T(8,128)(2,1)S(1)}, bf16[1,128,12288]{2,1,0:T(8,128)(2,1)}, u32[]{:S(2)}) copy-start(bf16[1,128,12288]{2,1,0:T(8,128)(2,1)} %param.5) | copy-start | bytes 9437188
  7.2 24.8 %copy-start.3 = (f32[1,12288]{1,0:T(1,128)S(1)}, f32[1,12288]{1,0:T(1,128)}, u32[]{:S(2)}) copy-start(f32[1,12288]{1,0:T(1,128)} %param.6) | copy-start | bytes 147460
  7.2 24.8 %all-gather.3.cloned.1.call-start = ((), (), s32[]{:S(2)}) async-start(), calls=%async_computation.1 | async-start | bytes 1966080 | tf_op jit(solution)/shard_map/all_gather | solution.py:23
  7.9 45.3 %all-gather.5.cloned.1.call-start = ((), (), s32[]{:S(2)}) async-start(), calls=%async_computation.2 | async-start | bytes 1966080 | tf_op jit(solution)/shard_map/all_gather | solution.py:40
  8.7 102.3 %reduce-scatter.2.cloned.1.call-start = ((), (), s32[]{:S(2)}) async-start(), calls=%async_computation.3 | async-start | bytes 1966080 | tf_op jit(solution)/shard_map/reduce_scatter | solution.py:48
  39.2 40.6 %copy-start.2 = (bf16[128,12288]{1,0:T(8,128)(2,1)S(1)}, bf16[128,12288]{1,0:T(8,128)(2,1)}, u32[]{:S(2)}) copy-start(bf16[128,12288]{1,0:T(8,128)(2,1)} %fusion.10) | copy-start | bytes 9437188
  81.6 31.3 %collective-permute-start = (bf16[128,64]{0,1:T(8,128)(2,1)S(1)}, bf16[128,64]{0,1:T(8,128)(2,1)S(1)}, u32[]{:S(2)}, u32[]{:S(2)}) collective-permute-start(bf16[128,64]{0,1:T(8,128)(2,1)S(1)} %convolution_convert_fusion.1), channel_id=1, source_target_pairs={{4,0},{8,4},{12,8},{16,12},{20,16},{24,20},{28,24},{5,1},{9,5},{13... | collective-permute-start | bytes 49160 | tf_op jit(solution)/shard_map/ppermute | solution.py:10
  111.0 13.0 %collective-permute-start.1 = (bf16[3072,64]{0,1:T(8,128)(2,1)}, bf16[3072,64]{0,1:T(8,128)(2,1)S(1)}, u32[]{:S(2)}, u32[]{:S(2)}) collective-permute-start(bf16[3072,64]{0,1:T(8,128)(2,1)} %reduce-scatter.2.cloned.1.call-done), channel_id=1, source_target_pairs={{4,0},{8,4},{12,8},{16,12},{20,16},{24,20},{28,24},{5,1},{9,5},{13... | collective-permute-start | bytes 1179656 | tf_op jit(solution)/shard_map/ppermute | solution.py:10
Sparse Core Ops, SparseCore 0:
  9.6 22.3 all-gather.2
  33.5 19.6 all-gather.4
  81.7 29.2 reduce-scatter.1
where the time goes:
time: 132 us
  waiting for transfers between devices  61.8 us (47%)
  blocking collectives  21 us (16%)
  other arithmetic  20.5 us (16%)
  between operations  13.9 us (11%)
  matrix products  9.86 us (7%)
  starting transfers between devices  2.69 us (2%)
  local copies, waits for them, and re-layouts  2.07 us (2%)
    all_gather x1, waiting for transfers between devices, on_device(): lax.all_gather(right_in, 'dp', axis=1, tiled=True)[0]  18 us
    reduce_scatter x1, waiting for transfers between devices, on_device(): lax.psum_scatter(jnp.dot(columns.T, ortho, preferred_element_type=jnp.flo...  17.4 us
    all_gather x1, waiting for transfers between devices, on_device(): lax.all_gather(basis, 'dp', axis=1, tiled=True)[0]  14 us
    ppermute x2, waiting for transfers between devices, shifted(): return lax.ppermute(x, axis, pairs)  11.1 us
    psum x1, blocking collectives, replica_sums(): totals = lax.psum(terms.astype(jnp.bfloat16), 'dp').astype(jnp.float32)  10.6 us
    psum x1, blocking collectives, on_device(): gram = lax.psum(gram_local, 'dp')  10.4 us
    another operation x3, other arithmetic, on_device(): lower = jnp.linalg.cholesky(gram)  6.52 us
    another operation x2, other arithmetic, on_device(): jax.scipy.linalg.solve_triangular(lower, power.T, lower=True)  5.55 us
  transfers between devices with their start and end apart: 5, of which 4 were waited for; matrix products, arithmetic and copies ran while one was open for 10% of the time, Pallas kernels for 0%

commit v1 on v0

v1 whole, which is shorter than its diff:
```python
import functools

import jax
import jax.numpy as jnp
from jax import lax
from jax.experimental import pallas as pl
from jax.experimental.pallas import tpu as pltpu
from jax.sharding import PartitionSpec as P

F32 = jnp.float32
BF16 = jnp.bfloat16
HIGH = lax.Precision.HIGHEST
NN = (((1,), (0,)), ((), ()))
NT = (((1,), (1,)), ((), ()))
LANES = 128
IN_PIECES = 3
OUT_PIECES = 6


def remote(src, dst, send, recv, **where):
    return pltpu.make_async_remote_copy(
        src_ref=src, dst_ref=dst, send_sem=send, recv_sem=recv,
        device_id=where, device_id_type=pl.DeviceIdType.MESH,
    )


def lane_tiles(v):
    total = v[:, :LANES]
    for i in range(1, v.shape[1] // LANES):
        total = total + v[:, i * LANES:(i + 1) * LANES]
    return total


def inverse_factor(gram):
    r, width = gram.shape
    row = lax.broadcasted_iota(jnp.int32, (r, width), 0)
    lane = lax.broadcasted_iota(jnp.int32, (r, width), 1)
    work = jnp.where(lane == row + r, 1.0, gram)
    done = []
    for j0 in range(0, r, 4):
        base = (j0 // 8) * 8
        o = j0 - base
        rows_here = lax.broadcasted_iota(jnp.int32, work.shape, 0)
        cols = [jnp.broadcast_to(work[:, j0 + k:j0 + k + 1], work.shape) for k in range(4)]
        rows = [work[o + k:o + k + 1, :] for k in range(4)]
        for k in range(4):
            scale = 1.0 / cols[k][o + k:o + k + 1, :]
            for m in range(k + 1, 4):
                f = cols[m][o + k:o + k + 1, :] * scale
                rows[m] = rows[m] - f * rows[k]
                cols[m] = cols[m] - cols[k] * f
            work = work - jnp.where(rows_here > o + k, cols[k], 0.0) * (rows[k] * scale)
        if o == 4:
            done.append(work[:8])
            work = work[8:]
    full = jnp.concatenate(done, axis=0)
    diagonal = jnp.sum(jnp.where(lane == row, full, 0.0), axis=1, keepdims=True)
    return full * lax.rsqrt(diagonal)


def kernel(
    n, sections, tokens_all,
    x_hbm, gain_ref, left_ref, r_hbm, b_hbm,
    gain_out, bias_out, left_out, right_out,
    x_v, rt, bt, scaled_v, bnd, acc1, acc2, terms, terms_in, grams, ortho_v,
    sib_out, sib_in, cross_out, cross_in, shift_v,
    local_sem, r_recv, r_cross, r_sib, r_fwd, b_recv, b_cross, b_sib, b_fwd,
    t_send, t_recv, g_send, g_recv, o_send, o_recv,
    s_send, s_recv, c_send, c_recv, f_send, f_recv,
):
    me = lax.axis_index("dp")
    section = lax.axis_index("section")
    chips = n // 2
    chip, core = me // 2, me % 2
    sib = chip * 2 + (1 - core)
    tokens, d = x_v.shape
    w = d // n
    pw = w // IN_PIECES
    ow = w // OUT_PIECES

    loads = [
        pltpu.make_async_copy(r_hbm, rt.at[me], local_sem.at[0]),
        pltpu.make_async_copy(x_hbm, x_v, local_sem.at[1]),
        pltpu.make_async_copy(b_hbm, bt.at[me], local_sem.at[2]),
    ]
    for load in loads:
        load.start()

    barrier = pltpu.get_barrier_semaphore()
    for i in range(1, n):
        pl.semaphore_signal(barrier, inc=1, device_id={"dp": (me + i) % n}, device_id_type=pl.DeviceIdType.MESH)

    @pl.when(section < sections - 1)
    def _():
        pl.semaphore_signal(barrier, inc=1, device_id={"section": section + 1}, device_id_type=pl.DeviceIdType.MESH)

    pl.semaphore_wait(barrier, jnp.where(section > 0, n, n - 1))

    def piece(p):
        return pl.ds(pl.multiple_of(p * pw, LANES), pw)

    def columns(j, p):
        return pl.ds(pl.multiple_of(j * w + p * pw, LANES), pw)

    def other(o):
        return ((chip + o) % chips) * 2 + core

    def source(o):
        return ((chip + chips - o) % chips) * 2 + core

    def flip(j):
        return j + 1 - 2 * core

    def to_cross(src, buf, recv, send, o, p):
        return remote(src.at[:, piece(p)], buf.at[me, :, piece(p)], send.at[o, p], recv.at[me, p], dp=other(o))

    def to_sib(src, buf, recv, send, p):
        return remote(src.at[:, piece(p)], buf.at[me, :, piece(p)], send.at[p], recv.at[me, p], dp=sib)

    def forward(buf, recv, send, o, p):
        j = source(o)
        return remote(buf.at[j, :, piece(p)], buf.at[j, :, piece(p)], send.at[o, p], recv.at[j, p], dp=sib)

    def arrived(buf, recv, send, j, p):
        remote(buf.at[j, :, piece(p)], buf.at[j, :, piece(p)], send.at[0], recv.at[j, p], dp=sib).wait_recv()

    for p in range(IN_PIECES):
        for o in range(1, chips):
            to_cross(r_hbm, rt, r_recv, r_cross, o, p).start()
    for p in range(IN_PIECES):
        to_sib(r_hbm, rt, r_recv, r_sib, p).start()

    step = d // 12
    loads[1].wait()

    def sum_step(i, acc):
        return acc + lane_tiles(x_v[:, pl.ds(pl.multiple_of(i * step, LANES), step)].astype(F32))

    zero = jnp.zeros((tokens, LANES), F32)
    mu = jnp.sum(lax.fori_loop(0, 12, sum_step, zero), axis=1, keepdims=True) / d

    def square_step(i, acc):
        c = x_v[:, pl.ds(pl.multiple_of(i * step, LANES), step)].astype(F32) - mu
        return acc + lane_tiles(c * c)

    var = jnp.sum(lax.fori_loop(0, 12, square_step, zero), axis=1, keepdims=True) / d
    inverse = lax.rsqrt(var + 1e-5)

    left = left_ref[...].astype(F32).T.astype(BF16)
    acc1[...] = zero
    acc2[...] = zero

    def first_pass(j, p):
        at = columns(j, p)
        rebuilt = lax.dot_general(left, rt[j, :, piece(p)], NN, preferred_element_type=F32)
        normed = (x_v[:, at].astype(F32) - mu) * inverse
        product = rebuilt * normed
        terms[j, 0:1, piece(p)] = jnp.sum(product, axis=0, keepdims=True)
        terms[j, 1:2, piece(p)] = jnp.sum(rebuilt, axis=0, keepdims=True)
        gain = gain_ref[:, at]
        scaled = rebuilt * gain
        scaled_v[:, at] = scaled
        acc1[...] += lane_tiles(scaled)
        acc2[...] += lane_tiles(product * gain)

    def loop(count, body):
        lax.fori_loop(0, count, lambda i, _: (body(i), 0)[1], 0)

    loads[0].wait()
    loop(IN_PIECES, lambda p: first_pass(me, p))

    def sib_first(p):
        arrived(rt, r_recv, r_sib, sib, p)
        first_pass(sib, p)

    loop(IN_PIECES, sib_first)

    def cross_first(i):
        p, o = i // (chips - 1), 1 + i % (chips - 1)
        arrived(rt, r_recv, r_sib, source(o), p)
        forward(rt, r_recv, r_fwd, o, p).start()
        to_cross(b_hbm, bt, b_recv, b_cross, o, p).start()
        first_pass(source(o), p)

    loop(IN_PIECES * (chips - 1), cross_first)
    loop(IN_PIECES, lambda p: to_sib(b_hbm, bt, b_recv, b_sib, p).start())

    def forwarded_first(i):
        p, o = i // (chips - 1), 1 + i % (chips - 1)
        arrived(rt, r_recv, r_sib, flip(source(o)), p)
        first_pass(flip(source(o)), p)

    loop(IN_PIECES * (chips - 1), forwarded_first)

    m1 = jnp.sum(acc1[...], axis=1, keepdims=True) / d * inverse
    m2 = jnp.sum(acc2[...], axis=1, keepdims=True) / d * inverse * inverse

    def second_pass(j, p):
        at = columns(j, p)
        center = x_v[:, at].astype(F32) - mu
        bnd[:, at] = (scaled_v[:, at] * inverse - m1 - center * m2).astype(BF16)

    def project(j, p):
        acc1[0:64, :] += lax.dot_general(bt[j, :, piece(p)], bnd[:, columns(j, p)], NT, preferred_element_type=F32)

    acc1[...] = zero
    loads[2].wait()

    def own_second(p):
        second_pass(me, p)
        project(me, p)

    loop(IN_PIECES, own_second)

    def sib_second(p):
        second_pass(sib, p)
        arrived(bt, b_recv, b_sib, sib, p)
        project(sib, p)

    loop(IN_PIECES, sib_second)

    def cross_second(i):
        p, o = i // (chips - 1), 1 + i % (chips - 1)
        second_pass(source(o), p)
        second_pass(flip(source(o)), p)
        arrived(bt, b_recv, b_sib, source(o), p)
        forward(bt, b_recv, b_fwd, o, p).start()
        project(source(o), p)

    loop(IN_PIECES * (chips - 1), cross_second)

    def forwarded_second(i):
        p, o = i // (chips - 1), 1 + i % (chips - 1)
        arrived(bt, b_recv, b_sib, flip(source(o)), p)
        project(flip(source(o)), p)

    loop(IN_PIECES * (chips - 1), forwarded_second)

    r = left_ref.shape[0]
    power = acc1[0:64, :]
    tall = jnp.concatenate([power, jnp.zeros_like(power)], axis=0)
    grams[me] = lax.dot_general(power, tall, NT, precision=HIGH, preferred_element_type=F32)

    def gram_copy(i):
        return remote(grams.at[me], grams.at[me], g_send.at[i], g_recv.at[me], dp=(me + i) % n)

    def terms_copy(i):
        to = (me + i) % n
        return remote(terms.at[to], terms_in.at[me], t_send.at[i], t_recv.at[me], dp=to)

    for i in range(1, n):
        gram_copy(i).start()
    for i in range(1, n):
        terms_copy(i).start()
    for i in range(1, n):
        j = (me + i) % n
        remote(grams.at[j], grams.at[j], g_send.at[0], g_recv.at[j], dp=sib).wait_recv()
    gram = grams[0]
    for j in range(1, n):
        gram = gram + grams[j]
    factor = inverse_factor(gram)
    low = jnp.concatenate([jnp.zeros_like(power), power], axis=0)
    ortho = lax.dot_general(factor, low, NN, precision=HIGH, preferred_element_type=F32).astype(BF16)
    ortho_v[...] = ortho

    def ortho_copy():
        return remote(ortho_v, left_out, o_send, o_recv, section=section - 1)

    @pl.when(section > 0)
    def _():
        ortho_copy().start()

    def out_piece(q):
        return pl.ds(pl.multiple_of(q * ow, LANES), ow)

    def share(j, q):
        at = pl.ds(pl.multiple_of(j * w + q * ow, LANES), ow)
        return lax.dot_general(ortho_v[...], bnd[:, at], NN, preferred_element_type=F32)

    def sib_copy(o, q):
        return remote(sib_out.at[o, :, out_piece(q)], sib_in.at[o, :, out_piece(q)], s_send.at[o, q], s_recv.at[o, q], dp=sib)

    def cross_copy(o, q):
        return remote(cross_out.at[o, :, out_piece(q)], cross_in.at[o, :, out_piece(q)], c_send.at[o, q], c_recv.at[o, q], dp=other(o))

    def shift_copy(q):
        return remote(shift_v.at[:, out_piece(q)], right_out.at[:, out_piece(q)], f_send.at[q], f_recv.at[q], section=section - 1)

    def send_sib(o, q):
        sib_out[o, :, out_piece(q)] = share(flip(other(o)), q).astype(BF16)
        sib_copy(o, q).start()

    def split(i):
        return 1 + i % (chips - 1), i // (chips - 1)

    def stage_a(i):
        o, q = split(i)
        send_sib(o, q)

    loop(OUT_PIECES * (chips - 1), stage_a)

    def stage_b(i):
        o, q = split(i)
        mine = share(other(o), q)
        sib_copy(o, q).wait_recv()
        cross_out[o, :, out_piece(q)] = (mine + sib_in[o, :, out_piece(q)].astype(F32)).astype(BF16)
        cross_copy(o, q).start()

    loop(OUT_PIECES * (chips - 1), stage_b)
    loop(OUT_PIECES, lambda q: send_sib(0, q))

    for i in range(1, n):
        j = (me + i) % n
        remote(terms.at[j], terms_in.at[j], t_send.at[0], t_recv.at[j], dp=sib).wait_recv()
    sums = terms[me]
    for i in range(1, n):
        sums = sums + terms_in[(me + i) % n]
    sums = sums * (1.0 / tokens_all ** 0.5)
    gain_out[...] = sums[0:1]
    bias_out[...] = sums[1:2]

    def stage_c(q):
        total = share(me, q)
        sib_copy(0, q).wait_recv()
        total = total + sib_in[0, :, out_piece(q)].astype(F32)
        for o in range(1, chips):
            cross_copy(o, q).wait_recv()
            total = total + cross_in[o, :, out_piece(q)].astype(F32)
        shift_v[:, out_piece(q)] = total.astype(BF16)

        @pl.when(section > 0)
        def _():
            shift_copy(q).start()

    loop(OUT_PIECES, stage_c)

    @pl.when(section == sections - 1)
    def _():
        left_out[...] = jnp.zeros_like(left_out)
        right_out[...] = jnp.zeros_like(right_out)

    def inputs_sent(i):
        p, o = i // (chips - 1), 1 + i % (chips - 1)
        to_cross(r_hbm, rt, r_recv, r_cross, o, p).wait_send()
        to_cross(b_hbm, bt, b_recv, b_cross, o, p).wait_send()
        forward(rt, r_recv, r_fwd, o, p).wait_send()
        forward(bt, b_recv, b_fwd, o, p).wait_send()

    loop(IN_PIECES * (chips - 1), inputs_sent)

    def inputs_sent_sib(p):
        to_sib(r_hbm, rt, r_recv, r_sib, p).wait_send()
        to_sib(b_hbm, bt, b_recv, b_sib, p).wait_send()

    loop(IN_PIECES, inputs_sent_sib)
    for i in range(1, n):
        gram_copy(i).wait_send()
        terms_copy(i).wait_send()

    def shares_sent(i):
        o, q = split(i)
        sib_copy(o, q).wait_send()
        cross_copy(o, q).wait_send()

    loop(OUT_PIECES * (chips - 1), shares_sent)
    loop(OUT_PIECES, lambda q: sib_copy(0, q).wait_send())

    @pl.when(section < sections - 1)
    def _():
        ortho_copy().wait_recv()
        loop(OUT_PIECES, lambda q: shift_copy(q).wait_recv())

    @pl.when(section > 0)
    def _():
        ortho_copy().wait_send()
        loop(OUT_PIECES, lambda q: shift_copy(q).wait_send())


def on_device(n, sections, saved_input, norm_gain, left_in, right_in, basis):
    _, tokens, d = saved_input.shape
    r = left_in.shape[2]
    w = d // n
    chips = n // 2
    vmem = pl.BlockSpec(memory_space=pltpu.VMEM)
    anywhere = pl.BlockSpec(memory_space=pl.ANY)
    dma = pltpu.SemaphoreType.DMA
    gather = [dma((n, IN_PIECES)), dma((chips, IN_PIECES)), dma((IN_PIECES,)), dma((chips, IN_PIECES))]
    gain, bias, left, right = pl.pallas_call(
        functools.partial(kernel, n, sections, tokens * n),
        out_shape=(
            jax.ShapeDtypeStruct((1, w), F32),
            jax.ShapeDtypeStruct((1, w), F32),
            jax.ShapeDtypeStruct((r, tokens), BF16),
            jax.ShapeDtypeStruct((r, w), BF16),
        ),
        in_specs=[anywhere, vmem, vmem, anywhere, anywhere],
        out_specs=(vmem, vmem, vmem, vmem),
        scratch_shapes=[
            pltpu.VMEM((tokens, d), BF16),
            pltpu.VMEM((n, r, w), BF16),
            pltpu.VMEM((n, r, w), BF16),
            pltpu.VMEM((tokens, d), F32),
            pltpu.VMEM((tokens, d), BF16),
            pltpu.VMEM((tokens, LANES), F32),
            pltpu.VMEM((tokens, LANES), F32),
            pltpu.VMEM((n, 2, w), F32),
            pltpu.VMEM((n, 2, w), F32),
            pltpu.VMEM((n, r, 2 * r), F32),
            pltpu.VMEM((r, tokens), BF16),
            pltpu.VMEM((chips, r, w), BF16),
            pltpu.VMEM((chips, r, w), BF16),
            pltpu.VMEM((chips, r, w), BF16),
            pltpu.VMEM((chips, r, w), BF16),
            pltpu.VMEM((r, w), BF16),
            dma((3,)),
            *gather,
            *gather,
            dma((n,)), dma((n,)),
            dma((n,)), dma((n,)),
            dma, dma,
            dma((chips, OUT_PIECES)), dma((chips, OUT_PIECES)),
            dma((chips, OUT_PIECES)), dma((chips, OUT_PIECES)),
            dma((OUT_PIECES,)), dma((OUT_PIECES,)),
        ],
        compiler_params=pltpu.CompilerParams(
            collective_id=0, has_side_effects=True, vmem_limit_bytes=48 * 1024 * 1024
        ),
    )(saved_input[0], norm_gain, left_in[0].T, right_in[0].T, basis[0].T)
    return gain, bias, left.T[None], right.T[None]


def solution(mesh):
    placed = (
        P("section", "dp", None),
        P("section", None),
        P("section", "dp", None),
        P("section", "dp", None),
        P("section", "dp", None),
    )
    return jax.shard_map(
        functools.partial(on_device, mesh.shape["dp"], mesh.shape["section"]),
        mesh=mesh,
        in_specs=placed,
        out_specs=(
            P("section", "dp"),
            P("section", "dp"),
            P("section", "dp", None),
            P("section", "dp", None),
        ),
        check_vma=False,
    )
```

time: 132 us -> 54.9 us (0.42)
  waiting for transfers between devices: 61.8 us -> 0 us
  Pallas kernels: 0 us -> 46 us
  blocking collectives: 21 us -> 0 us
  other arithmetic: 20.5 us -> 0 us
  between operations: 13.9 us -> 0.65 us
  matrix products: 9.86 us -> 0 us
  local copies, waits for them, and re-layouts: 2.07 us -> 7.94 us
  starting transfers between devices: 2.69 us -> 0 us
    pallas_call x0 -> x1, Pallas kernels: none -> 46 us  [on_device(): pl.pallas_call(functools.partial(kernel, n, sections, tokens * n), out_sh...]
    all_gather x2 -> x0, waiting for transfers between devices: 32 us -> none  [the longest x1 18 us: on_device(): lax.all_gather(right_in, 'dp', axis=1, tiled=True)[0]]
    psum x2 -> x0, blocking collectives: 21 us -> none  [the longest x1 10.6 us: replica_sums(): totals = lax.psum(terms.astype(jnp.bfloat16), 'dp').astype(jnp.float32)]
    reduce_scatter x1 -> x0, waiting for transfers between devices: 17.4 us -> none  [on_device(): lax.psum_scatter(jnp.dot(columns.T, ortho, preferred_element_type=jnp.flo...]
    another operation x5 -> x0, other arithmetic: 12.1 us -> none  [the longest x3 6.52 us: on_device(): lower = jnp.linalg.cholesky(gram)]
    ppermute x2 -> x0, waiting for transfers between devices: 11.1 us -> none  [shifted(): return lax.ppermute(x, axis, pairs)]
    dot_general x4 -> x0, matrix products: 9.61 us -> none  [the longest x1 4.15 us: on_device(): jnp.dot(left, lax.all_gather(right_in, 'dp', axis=1, tiled=True)[0].T, pr...]
    unnamed x10 -> x14, local copies, waits for them, and re-layouts: 1.37 us -> 7.94 us
  transfers between devices with their start and end apart: 5 -> 0, of which waited for: 4 -> 0; matrix products, arithmetic and copies ran while one was open for 10% -> 0% of each run, Pallas kernels for 0% -> 0%
where the time goes in v1:
time: 54.9 us; the launch traced here: 54.6 us
  Pallas kernels  46 us (84%)
  local copies, waits for them, and re-layouts  7.94 us (14%)
  between operations  0.65 us (1%)
    pallas_call x1, Pallas kernels, on_device(): pl.pallas_call(functools.partial(kernel, n, sections, tokens * n), out_sh...  46 us
    unnamed x14, local copies, waits for them, and re-layouts  7.94 us

profile of v1, /device:TPU:0, one launch (start us, length us, event | category | flops | bytes accessed | tf_op | source)
XLA Modules:
  0.0 54.6 jit_solution(16063305608744008876)
XLA Ops:
  0.6 0.0 copy-start
  0.6 1.9 %copy-done = bf16[1,128,12288]{2,1,0:T(8,128)(2,1)S(1)} copy-done((bf16[1,128,12288]{2,1,0:T(8,128)(2,1)S(1)}, bf16[1,128,12288]{2,1,0:T(8,128)(2,1)}, u32[]{:S(2)}) %copy-start) | copy-done | bytes 3145752
  2.5 0.0 copy-start.1
  2.5 1.0 %copy-done.1 = bf16[1,3072,64]{1,2,0:T(8,128)(2,1)S(1)} copy-done((bf16[1,3072,64]{1,2,0:T(8,128)(2,1)S(1)}, bf16[1,3072,64]{1,2,0:T(8,128)(2,1)}, u32[]{:S(2)}) %copy-start.1) | copy-done | bytes 393240
  3.5 0.0 copy-start.2
  3.5 1.0 %copy-done.2 = bf16[1,3072,64]{1,2,0:T(8,128)(2,1)S(1)} copy-done((bf16[1,3072,64]{1,2,0:T(8,128)(2,1)S(1)}, bf16[1,3072,64]{1,2,0:T(8,128)(2,1)}, u32[]{:S(2)}) %copy-start.2) | copy-done | bytes 393240
  4.5 0.0 copy-start.3
  4.5 0.8 %copy-done.3 = f32[1,12288]{1,0:T(1,128)S(1)} copy-done((f32[1,12288]{1,0:T(1,128)S(1)}, f32[1,12288]{1,0:T(1,128)}, u32[]{:S(2)}) %copy-start.3) | copy-done | bytes 49176
  5.3 0.0 copy-start.4
  5.3 0.7 %copy-done.4 = bf16[1,128,64]{1,2,0:T(8,128)(2,1)S(1)} copy-done((bf16[1,128,64]{1,2,0:T(8,128)(2,1)S(1)}, bf16[1,128,64]{1,2,0:T(8,128)(2,1)}, u32[]{:S(2)}) %copy-start.4) | copy-done | bytes 16408
  6.0 46.0 %shard_map.84 = (f32[1,3072]{1,0:T(1,128)S(1)}, f32[1,3072]{1,0:T(1,128)S(1)}, bf16[64,128]{1,0:T(8,128)(2,1)S(1)}, bf16[64,3072]{1,0:T(8,128)(2,1)S(1)}) custom-call(bf16[128,12288]{1,0:T(8,128)(2,1)S(1)} %bitcast.16, f32[1,12288]{1,0:T(1,128)S(1)} %copy-done.3, bf16[64,128]{1,0:T(8,128)(2,1)S(1)} %bitcast.20, bf16[64,3072]{1,0:T(8,128)(2,1)S(1)} %bitcast.18, ...), custom_call_target="tpu_custom_call" | custom-call | tf_op jit(solution)/shard_map/pallas_call | solution.py:388
  52.0 0.6 %copy.13 = f32[1,3072]{1,0:T(1,128)} copy(f32[1,3072]{1,0:T(1,128)S(1)} %get-tuple-element.16) | data formatting | bytes 24576
  52.6 0.6 %copy.14 = f32[1,3072]{1,0:T(1,128)} copy(f32[1,3072]{1,0:T(1,128)S(1)} %get-tuple-element.17) | data formatting | bytes 24576
  53.2 0.6 %copy.15 = bf16[1,128,64]{1,2,0:T(8,128)(2,1)} copy(bf16[1,128,64]{1,2,0:T(8,128)(2,1)S(1)} %bitcast.21) | data formatting | bytes 32768
  53.8 0.7 %copy.16 = bf16[1,3072,64]{1,2,0:T(8,128)(2,1)} copy(bf16[1,3072,64]{1,2,0:T(8,128)(2,1)S(1)} %bitcast.17) | data formatting | bytes 786432
Async XLA Ops:
  0.6 1.9 %copy-start = (bf16[1,128,12288]{2,1,0:T(8,128)(2,1)S(1)}, bf16[1,128,12288]{2,1,0:T(8,128)(2,1)}, u32[]{:S(2)}) copy-start(bf16[1,128,12288]{2,1,0:T(8,128)(2,1)} %param.5) | copy-start | bytes 9437188
  2.5 1.0 %copy-start.1 = (bf16[1,3072,64]{1,2,0:T(8,128)(2,1)S(1)}, bf16[1,3072,64]{1,2,0:T(8,128)(2,1)}, u32[]{:S(2)}) copy-start(bf16[1,3072,64]{1,2,0:T(8,128)(2,1)} %param.8) | copy-start | bytes 1179652
  3.5 1.0 %copy-start.2 = (bf16[1,3072,64]{1,2,0:T(8,128)(2,1)S(1)}, bf16[1,3072,64]{1,2,0:T(8,128)(2,1)}, u32[]{:S(2)}) copy-start(bf16[1,3072,64]{1,2,0:T(8,128)(2,1)} %param.9) | copy-start | bytes 1179652
  4.5 0.8 %copy-start.3 = (f32[1,12288]{1,0:T(1,128)S(1)}, f32[1,12288]{1,0:T(1,128)}, u32[]{:S(2)}) copy-start(f32[1,12288]{1,0:T(1,128)} %gain_ref.1) | copy-start | bytes 147460
  5.3 0.7 %copy-start.4 = (bf16[1,128,64]{1,2,0:T(8,128)(2,1)S(1)}, bf16[1,128,64]{1,2,0:T(8,128)(2,1)}, u32[]{:S(2)}) copy-start(bf16[1,128,64]{1,2,0:T(8,128)(2,1)} %param.7) | copy-start | bytes 49156

commit v2 on v1

--- a/solution.py
+++ b/solution.py
@@ -60,9 +60,9 @@
 
 def kernel(
     n, sections, tokens_all,
-    x_hbm, gain_ref, left_ref, r_hbm, b_hbm,
+    x_hbm, gain_hbm, left_hbm, r_hbm, b_hbm,
     gain_out, bias_out, left_out, right_out,
-    x_v, rt, bt, scaled_v, bnd, acc1, acc2, terms, terms_in, grams, ortho_v,
+    gain_ref, left_ref, x_v, rt, bt, scaled_v, bnd, acc1, acc2, terms, terms_in, grams, ortho_v,
     sib_out, sib_in, cross_out, cross_in, shift_v,
     local_sem, r_recv, r_cross, r_sib, r_fwd, b_recv, b_cross, b_sib, b_fwd,
     t_send, t_recv, g_send, g_recv, o_send, o_recv,
@@ -82,6 +82,8 @@
         pltpu.make_async_copy(r_hbm, rt.at[me], local_sem.at[0]),
         pltpu.make_async_copy(x_hbm, x_v, local_sem.at[1]),
         pltpu.make_async_copy(b_hbm, bt.at[me], local_sem.at[2]),
+        pltpu.make_async_copy(gain_hbm, gain_ref, local_sem.at[3]),
+        pltpu.make_async_copy(left_hbm, left_ref, local_sem.at[4]),
     ]
     for load in loads:
         load.start()
@@ -146,6 +148,7 @@
     var = jnp.sum(lax.fori_loop(0, 12, square_step, zero), axis=1, keepdims=True) / d
     inverse = lax.rsqrt(var + 1e-5)
 
+    loads[4].wait()
     left = left_ref[...].astype(F32).T.astype(BF16)
     acc1[...] = zero
     acc2[...] = zero
@@ -167,6 +170,7 @@
         lax.fori_loop(0, count, lambda i, _: (body(i), 0)[1], 0)
 
     loads[0].wait()
+    loads[3].wait()
     loop(IN_PIECES, lambda p: first_pass(me, p))
 
     def sib_first(p):
@@ -376,26 +380,37 @@
         loop(OUT_PIECES, lambda q: shift_copy(q).wait_send())
 
 
+def write_out(*refs):
+    copies = [pltpu.make_async_copy(refs[i], refs[4 + i], refs[8].at[i]) for i in range(4)]
+    for copy in copies:
+        copy.start()
+    for copy in copies:
+        copy.wait()
+
+
 def on_device(n, sections, saved_input, norm_gain, left_in, right_in, basis):
     _, tokens, d = saved_input.shape
     r = left_in.shape[2]
     w = d // n
     chips = n // 2
     vmem = pl.BlockSpec(memory_space=pltpu.VMEM)
-    anywhere = pl.BlockSpec(memory_space=pl.ANY)
+    hbm = pl.BlockSpec(memory_space=pltpu.HBM)
     dma = pltpu.SemaphoreType.DMA
     gather = [dma((n, IN_PIECES)), dma((chips, IN_PIECES)), dma((IN_PIECES,)), dma((chips, IN_PIECES))]
-    gain, bias, left, right = pl.pallas_call(
+    results = (
+        jax.ShapeDtypeStruct((1, w), F32),
+        jax.ShapeDtypeStruct((1, w), F32),
+        jax.ShapeDtypeStruct((r, tokens), BF16),
+        jax.ShapeDtypeStruct((r, w), BF16),
+    )
+    held = pl.pallas_call(
         functools.partial(kernel, n, sections, tokens * n),
-        out_shape=(
-            jax.ShapeDtypeStruct((1, w), F32),
-            jax.ShapeDtypeStruct((1, w), F32),
-            jax.ShapeDtypeStruct((r, tokens), BF16),
-            jax.ShapeDtypeStruct((r, w), BF16),
-        ),
-        in_specs=[anywhere, vmem, vmem, anywhere, anywhere],
+        out_shape=results,
+        in_specs=[hbm] * 5,
         out_specs=(vmem, vmem, vmem, vmem),
         scratch_shapes=[
+            pltpu.VMEM((1, d), F32),
+            pltpu.VMEM((r, tokens), BF16),
             pltpu.VMEM((tokens, d), BF16),
             pltpu.VMEM((n, r, w), BF16),
             pltpu.VMEM((n, r, w), BF16),
@@ -412,7 +427,7 @@
             pltpu.VMEM((chips, r, w), BF16),
             pltpu.VMEM((chips, r, w), BF16),
             pltpu.VMEM((r, w), BF16),
-            dma((3,)),
+            dma((5,)),
             *gather,
             *gather,
             dma((n,)), dma((n,)),
@@ -423,9 +438,17 @@
             dma((OUT_PIECES,)), dma((OUT_PIECES,)),
         ],
         compiler_params=pltpu.CompilerParams(
-            collective_id=0, has_side_effects=True, vmem_limit_bytes=48 * 1024 * 1024
+            collective_id=0, has_side_effects=True, vmem_limit_bytes=63 * 1024 * 1024
         ),
     )(saved_input[0], norm_gain, left_in[0].T, right_in[0].T, basis[0].T)
+    gain, bias, left, right = pl.pallas_call(
+        write_out,
+        out_shape=results,
+        in_specs=[hbm] * 4,
+        out_specs=(hbm,) * 4,
+        scratch_shapes=[dma((4,))],
+        compiler_params=pltpu.CompilerParams(vmem_limit_bytes=63 * 1024 * 1024),
+    )(*held)
     return gain, bias, left.T[None], right.T[None]
 
 

time: 54.9 us -> 61.5 us (1.12)
  Pallas kernels: 46 us -> 60.7 us
  local copies, waits for them, and re-layouts: 7.94 us -> 0 us
    pallas_call x0 -> x1, Pallas kernels: none -> 14.3 us  [on_device(): pl.pallas_call(write_out, out_shape=results, in_specs=[hbm] * 4, out_spec...]
    unnamed x14 -> x0, local copies, waits for them, and re-layouts: 7.94 us -> none
where the time goes in v2:
time: 61.5 us; the launch traced here: 61.3 us
  Pallas kernels  60.7 us (99%)
  between operations  0.64 us (1%)
    pallas_call x1, Pallas kernels, on_device(): pl.pallas_call(functools.partial(kernel, n, sections, tokens * n), out_sh...  46.4 us
    pallas_call x1, Pallas kernels, on_device(): pl.pallas_call(write_out, out_shape=results, in_specs=[hbm] * 4, out_spec...  14.3 us

profile of v2, /device:TPU:0, one launch (start us, length us, event | category | flops | bytes accessed | tf_op | source)
XLA Modules:
  0.0 61.3 jit_solution(14477795541222560147)
XLA Ops:
  0.6 46.4 %shard_map.84 = (f32[1,3072]{1,0:T(1,128)}, f32[1,3072]{1,0:T(1,128)}, bf16[64,128]{1,0:T(8,128)(2,1)}, bf16[64,3072]{1,0:T(8,128)(2,1)}) custom-call(bf16[128,12288]{1,0:T(8,128)(2,1)} %bitcast.16, f32[1,12288]{1,0:T(1,128)} %gain_hbm.1, bf16[64,128]{1,0:T(8,128)(2,1)} %bitcast.19, bf16[64,3072]{1,0:T(8,128)(2,1)} %bitcast.17, bf16[64,3072]{1,0:T(8,128)(2,1)} %bitcast.18), custom_call_target="tpu_custom_call" | custom-call | tf_op jit(solution)/shard_map/pallas_call | solution.py:406
  47.0 14.3 %shard_map.85 = (f32[1,3072]{1,0:T(1,128)}, f32[1,3072]{1,0:T(1,128)}, bf16[64,128]{1,0:T(8,128)(2,1)}, bf16[64,3072]{1,0:T(8,128)(2,1)}) custom-call(f32[1,3072]{1,0:T(1,128)} %get-tuple-element.12.refs_0_, f32[1,3072]{1,0:T(1,128)} %get-tuple-element.13.refs_1_, bf16[64,128]{1,0:T(8,128)(2,1)} %get-tuple-element.14.refs_2_, ...), custom_call_target="tpu_custom_call" | custom-call | tf_op jit(solution)/shard_map/pallas_call | solution.py:444

commit v3 on v2

--- a/solution.py
+++ b/solution.py
@@ -35,7 +35,7 @@
     r, width = gram.shape
     row = lax.broadcasted_iota(jnp.int32, (r, width), 0)
     lane = lax.broadcasted_iota(jnp.int32, (r, width), 1)
-    work = jnp.where(lane == row + r, 1.0, gram)
+    work = jnp.where(lane < r, gram, jnp.where(lane == row + r, 1.0, 0.0))
     done = []
     for j0 in range(0, r, 4):
         base = (j0 // 8) * 8
@@ -62,10 +62,10 @@
     n, sections, tokens_all,
     x_hbm, gain_hbm, left_hbm, r_hbm, b_hbm,
     gain_out, bias_out, left_out, right_out,
-    gain_ref, left_ref, x_v, rt, bt, scaled_v, bnd, acc1, acc2, terms, terms_in, grams, ortho_v,
+    gain_ref, left_ref, x_v, rt, bt, scaled_v, bnd, acc1, acc2, terms, terms_in, grams, ortho_v, power_v, pre, conditioner,
     sib_out, sib_in, cross_out, cross_in, shift_v,
     local_sem, r_recv, r_cross, r_sib, r_fwd, b_recv, b_cross, b_sib, b_fwd,
-    t_send, t_recv, g_send, g_recv, o_send, o_recv,
+    p_send, p_recv, t_send, t_recv, g_send, g_recv, o_send, o_recv,
     s_send, s_recv, c_send, c_recv, f_send, f_recv,
 ):
     me = lax.axis_index("dp")
@@ -152,6 +152,40 @@
     left = left_ref[...].astype(F32).T.astype(BF16)
     acc1[...] = zero
     acc2[...] = zero
+
+    loads[0].wait()
+    loads[2].wait()
+    loads[3].wait()
+    r = left_ref.shape[0]
+
+    def stack(top, bottom):
+        return jnp.concatenate([top, bottom], axis=0)
+
+    def moments(p, carry):
+        product, sums = carry
+        scaled = rt[me, :, piece(p)].astype(F32) * gain_ref[:, columns(me, p)]
+        high = scaled.astype(BF16)
+        low = (scaled - high.astype(F32)).astype(BF16)
+        both = bt[me, :, piece(p)]
+        nothing = jnp.zeros_like(both)
+        ones = jnp.ones((16, pw), BF16)
+        right = stack(both, nothing)
+        for part in (high, low):
+            product = product + lax.dot_general(part, right, NT, preferred_element_type=F32)
+            sums = sums + lax.dot_general(ones, stack(nothing, part), NT, preferred_element_type=F32)
+        return product, sums + lax.dot_general(ones, right, NT, preferred_element_type=F32)
+
+    product, sums = lax.fori_loop(0, IN_PIECES, moments, (jnp.zeros((r, 2 * r), F32), jnp.zeros((16, 2 * r), F32)))
+    weighted = (left.astype(F32) * inverse).T
+    spread = lax.dot_general(weighted, stack(jnp.zeros_like(weighted), weighted), NT, precision=HIGH, preferred_element_type=F32)
+    pre[me, 0:r, :] = product + spread
+    pre[me, r:r + 8, :] = sums[0:8]
+
+    def pre_copy(i):
+        return remote(pre.at[me], pre.at[me], p_send.at[i], p_recv.at[me], dp=(me + i) % n)
+
+    for i in range(1, n):
+        pre_copy(i).start()
 
     def first_pass(j, p):
         at = columns(j, p)
@@ -169,8 +203,6 @@
     def loop(count, body):
         lax.fori_loop(0, count, lambda i, _: (body(i), 0)[1], 0)
 
-    loads[0].wait()
-    loads[3].wait()
     loop(IN_PIECES, lambda p: first_pass(me, p))
 
     def sib_first(p):
@@ -189,6 +221,26 @@
     loop(IN_PIECES * (chips - 1), cross_first)
     loop(IN_PIECES, lambda p: to_sib(b_hbm, bt, b_recv, b_sib, p).start())
 
+    for i in range(1, n):
+        j = (me + i) % n
+        remote(pre.at[j], pre.at[j], p_send.at[0], p_recv.at[j], dp=sib).wait_recv()
+    whole = pre[0]
+    for j in range(1, n):
+        whole = whole + pre[j]
+    tile, sums = whole[0:r], whole[r:r + 8]
+    row = lax.broadcasted_iota(jnp.int32, (r, 2 * r), 0)
+    lane = lax.broadcasted_iota(jnp.int32, (r, 2 * r), 1)
+    pick = jnp.where(lane == row + r, 1.0, 0.0)
+    r_sums = lax.dot_general(pick, sums, NT, precision=HIGH, preferred_element_type=F32)
+    b_sums = jnp.where(lane[0:8] < r, sums, 0.0) * (1.0 / (8 * d))
+    moment = jnp.where(lane < r, tile, 0.0) - lax.dot_general(r_sums, b_sums, NN, precision=HIGH, preferred_element_type=F32)
+    moved = lax.dot_general(tile[:, r:], moment, NN, precision=HIGH, preferred_element_type=F32)
+    turned = moment.T[0:r]
+    guess = lax.dot_general(turned, moved, NN, precision=HIGH, preferred_element_type=F32)
+    diagonal = jnp.where(lane == row, guess, 0.0)
+    level = jnp.sum(jnp.sum(diagonal, axis=1, keepdims=True), axis=0, keepdims=True) * (1e-4 / r) + 1e-30
+    conditioner[...] = inverse_factor(guess + jnp.where(lane == row, level, 0.0))
+
     def forwarded_first(i):
         p, o = i // (chips - 1), 1 + i % (chips - 1)
         arrived(rt, r_recv, r_sib, flip(source(o)), p)
@@ -205,10 +257,9 @@
         bnd[:, at] = (scaled_v[:, at] * inverse - m1 - center * m2).astype(BF16)
 
     def project(j, p):
-        acc1[0:64, :] += lax.dot_general(bt[j, :, piece(p)], bnd[:, columns(j, p)], NT, preferred_element_type=F32)
+        acc1[0:r, :] += lax.dot_general(bt[j, :, piece(p)], bnd[:, columns(j, p)], NT, preferred_element_type=F32)
 
     acc1[...] = zero
-    loads[2].wait()
 
     def own_second(p):
         second_pass(me, p)
@@ -240,10 +291,44 @@
 
     loop(IN_PIECES * (chips - 1), forwarded_second)
 
-    r = left_ref.shape[0]
-    power = acc1[0:64, :]
-    tall = jnp.concatenate([power, jnp.zeros_like(power)], axis=0)
-    grams[me] = lax.dot_general(power, tall, NT, precision=HIGH, preferred_element_type=F32)
+    plain = acc1[0:r, :]
+    power = lax.dot_general(conditioner[...], stack(jnp.zeros_like(plain), plain), NN, precision=HIGH, preferred_element_type=F32)
+    power_v[...] = power.astype(BF16)
+
+    def out_piece(q):
+        return pl.ds(pl.multiple_of(q * ow, LANES), ow)
+
+    def share(j, q):
+        at = pl.ds(pl.multiple_of(j * w + q * ow, LANES), ow)
+        return lax.dot_general(power_v[...], bnd[:, at], NN, preferred_element_type=F32)
+
+    def sib_copy(o, q):
+        return remote(sib_out.at[o, :, out_piece(q)], sib_in.at[o, :, out_piece(q)], s_send.at[o, q], s_recv.at[o, q], dp=sib)
+
+    def cross_copy(o, q):
+        return remote(cross_out.at[o, :, out_piece(q)], cross_in.at[o, :, out_piece(q)], c_send.at[o, q], c_recv.at[o, q], dp=other(o))
+
+    def shift_copy(q):
+        return remote(shift_v.at[:, out_piece(q)], right_out.at[:, out_piece(q)], f_send.at[q], f_recv.at[q], section=section - 1)
+
+    def send_sib(o, q):
+        sib_out[o, :, out_piece(q)] = share(flip(other(o)), q).astype(BF16)
+        sib_copy(o, q).start()
+
+    def split(i):
+        return 1 + i % (chips - 1), i // (chips - 1)
+
+    def stage_a(i):
+        o, q = split(i)
+        send_sib(o, q)
+
+    loop(OUT_PIECES * (chips - 1), stage_a)
+
+    half = r // 2
+    nothing = jnp.zeros_like(power)
+    grams[me] = lax.dot_general(
+        power[0:half], stack(power, nothing), NT, precision=HIGH, preferred_element_type=F32
+    ) + lax.dot_general(power[half:r], stack(nothing, power), NT, precision=HIGH, preferred_element_type=F32)
 
     def gram_copy(i):
         return remote(grams.at[me], grams.at[me], g_send.at[i], g_recv.at[me], dp=(me + i) % n)
@@ -254,54 +339,6 @@
 
     for i in range(1, n):
         gram_copy(i).start()
-    for i in range(1, n):
-        terms_copy(i).start()
-    for i in range(1, n):
-        j = (me + i) % n
-        remote(grams.at[j], grams.at[j], g_send.at[0], g_recv.at[j], dp=sib).wait_recv()
-    gram = grams[0]
-    for j in range(1, n):
-        gram = gram + grams[j]
-    factor = inverse_factor(gram)
-    low = jnp.concatenate([jnp.zeros_like(power), power], axis=0)
-    ortho = lax.dot_general(factor, low, NN, precision=HIGH, preferred_element_type=F32).astype(BF16)
-    ortho_v[...] = ortho
-
-    def ortho_copy():
-        return remote(ortho_v, left_out, o_send, o_recv, section=section - 1)
-
-    @pl.when(section > 0)
-    def _():
-        ortho_copy().start()
-
-    def out_piece(q):
-        return pl.ds(pl.multiple_of(q * ow, LANES), ow)
-
-    def share(j, q):
-        at = pl.ds(pl.multiple_of(j * w + q * ow, LANES), ow)
-        return lax.dot_general(ortho_v[...], bnd[:, at], NN, preferred_element_type=F32)
-
-    def sib_copy(o, q):
-        return remote(sib_out.at[o, :, out_piece(q)], sib_in.at[o, :, out_piece(q)], s_send.at[o, q], s_recv.at[o, q], dp=sib)
-
-    def cross_copy(o, q):
-        return remote(cross_out.at[o, :, out_piece(q)], cross_in.at[o, :, out_piece(q)], c_send.at[o, q], c_recv.at[o, q], dp=other(o))
-
-    def shift_copy(q):
-        return remote(shift_v.at[:, out_piece(q)], right_out.at[:, out_piece(q)], f_send.at[q], f_recv.at[q], section=section - 1)
-
-    def send_sib(o, q):
-        sib_out[o, :, out_piece(q)] = share(flip(other(o)), q).astype(BF16)
-        sib_copy(o, q).start()
-
-    def split(i):
-        return 1 + i % (chips - 1), i // (chips - 1)
-
-    def stage_a(i):
-        o, q = split(i)
-        send_sib(o, q)
-
-    loop(OUT_PIECES * (chips - 1), stage_a)
 
     def stage_b(i):
         o, q = split(i)
@@ -312,6 +349,25 @@
 
     loop(OUT_PIECES * (chips - 1), stage_b)
     loop(OUT_PIECES, lambda q: send_sib(0, q))
+
+    for i in range(1, n):
+        terms_copy(i).start()
+    for i in range(1, n):
+        j = (me + i) % n
+        remote(grams.at[j], grams.at[j], g_send.at[0], g_recv.at[j], dp=sib).wait_recv()
+    packed = grams[0]
+    for j in range(1, n):
+        packed = packed + grams[j]
+    factor = inverse_factor(stack(packed, pltpu.roll(packed, r, 1)))
+    conditioner[...] = factor
+    ortho_v[...] = lax.dot_general(factor, stack(nothing, power), NN, precision=HIGH, preferred_element_type=F32).astype(BF16)
+
+    def ortho_copy():
+        return remote(ortho_v, left_out, o_send, o_recv, section=section - 1)
+
+    @pl.when(section > 0)
+    def _():
+        ortho_copy().start()
 
     for i in range(1, n):
         j = (me + i) % n
@@ -330,6 +386,7 @@
         for o in range(1, chips):
             cross_copy(o, q).wait_recv()
             total = total + cross_in[o, :, out_piece(q)].astype(F32)
+        total = lax.dot_general(conditioner[...], stack(jnp.zeros_like(total), total), NN, precision=HIGH, preferred_element_type=F32)
         shift_v[:, out_piece(q)] = total.astype(BF16)
 
         @pl.when(section > 0)
@@ -360,6 +417,7 @@
     for i in range(1, n):
         gram_copy(i).wait_send()
         terms_copy(i).wait_send()
+        pre_copy(i).wait_send()
 
     def shares_sent(i):
         o, q = split(i)
@@ -381,10 +439,14 @@
 
 
 def write_out(*refs):
-    copies = [pltpu.make_async_copy(refs[i], refs[4 + i], refs[8].at[i]) for i in range(4)]
-    for copy in copies:
+    come = [pltpu.make_async_copy(refs[i], refs[8 + i], refs[12].at[i]) for i in range(4)]
+    go = [pltpu.make_async_copy(refs[8 + i], refs[4 + i], refs[13].at[i]) for i in range(4)]
+    for copy in come:
         copy.start()
-    for copy in copies:
+    for first, second in zip(come, go):
+        first.wait()
+        second.start()
+    for copy in go:
         copy.wait()
 
 
@@ -420,8 +482,11 @@
             pltpu.VMEM((tokens, LANES), F32),
             pltpu.VMEM((n, 2, w), F32),
             pltpu.VMEM((n, 2, w), F32),
-            pltpu.VMEM((n, r, 2 * r), F32),
+            pltpu.VMEM((n, r // 2, 2 * r), F32),
             pltpu.VMEM((r, tokens), BF16),
+            pltpu.VMEM((r, tokens), BF16),
+            pltpu.VMEM((n, r + 8, 2 * r), F32),
+            pltpu.VMEM((r, 2 * r), F32),
             pltpu.VMEM((chips, r, w), BF16),
             pltpu.VMEM((chips, r, w), BF16),
             pltpu.VMEM((chips, r, w), BF16),
@@ -430,6 +495,7 @@
             dma((5,)),
             *gather,
             *gather,
+            dma((n,)), dma((n,)),
             dma((n,)), dma((n,)),
             dma((n,)), dma((n,)),
             dma, dma,
@@ -446,7 +512,7 @@
         out_shape=results,
         in_specs=[hbm] * 4,
         out_specs=(hbm,) * 4,
-        scratch_shapes=[dma((4,))],
+        scratch_shapes=[*(pltpu.VMEM(a.shape, a.dtype) for a in results), dma((4,)), dma((4,))],
         compiler_params=pltpu.CompilerParams(vmem_limit_bytes=63 * 1024 * 1024),
     )(*held)
     return gain, bias, left.T[None], right.T[None]

time: 61.5 us -> 54.4 us (0.88)
  Pallas kernels: 60.7 us -> 53.5 us
    pallas_call x1, Pallas kernels: 14.3 us -> 1.86 us  [on_device(): pl.pallas_call(write_out, out_shape=results, in_specs=[hbm] * 4, out_spec...]
    pallas_call x1, Pallas kernels: 46.4 us -> 51.7 us  [on_device(): pl.pallas_call(functools.partial(kernel, n, sections, tokens * n), out_sh...]
where the time goes in v3:
time: 54.4 us; the launch traced here: 54.2 us
  Pallas kernels  53.5 us (98%)
  between operations  0.64 us (1%)
    pallas_call x1, Pallas kernels, on_device(): pl.pallas_call(functools.partial(kernel, n, sections, tokens * n), out_sh...  51.7 us
    pallas_call x1, Pallas kernels, on_device(): pl.pallas_call(write_out, out_shape=results, in_specs=[hbm] * 4, out_spec...  1.86 us

profile of v3, /device:TPU:0, one launch (start us, length us, event | category | flops | bytes accessed | tf_op | source)
XLA Modules:
  0.0 54.2 jit_solution(12767789993557407750)
XLA Ops:
  0.6 51.7 %shard_map.84 = (f32[1,3072]{1,0:T(1,128)}, f32[1,3072]{1,0:T(1,128)}, bf16[64,128]{1,0:T(8,128)(2,1)}, bf16[64,3072]{1,0:T(8,128)(2,1)}) custom-call(bf16[128,12288]{1,0:T(8,128)(2,1)} %bitcast.16, f32[1,12288]{1,0:T(1,128)} %gain_hbm.1, bf16[64,128]{1,0:T(8,128)(2,1)} %bitcast.19, bf16[64,3072]{1,0:T(8,128)(2,1)} %bitcast.17, bf16[64,3072]{1,0:T(8,128)(2,1)} %bitcast.18), custom_call_target="tpu_custom_call" | custom-call | tf_op jit(solution)/shard_map/pallas_call | solution.py:468
  52.3 1.9 %shard_map.85 = (f32[1,3072]{1,0:T(1,128)}, f32[1,3072]{1,0:T(1,128)}, bf16[64,128]{1,0:T(8,128)(2,1)}, bf16[64,3072]{1,0:T(8,128)(2,1)}) custom-call(f32[1,3072]{1,0:T(1,128)} %get-tuple-element.12.refs_0_, f32[1,3072]{1,0:T(1,128)} %get-tuple-element.13.refs_1_, bf16[64,128]{1,0:T(8,128)(2,1)} %get-tuple-element.14.refs_2_, ...), custom_call_target="tpu_custom_call" | custom-call | tf_op jit(solution)/shard_map/pallas_call | solution.py:510

commit v4 on v2

--- a/solution.py
+++ b/solution.py
@@ -15,6 +15,8 @@
 LANES = 128
 IN_PIECES = 3
 OUT_PIECES = 6
+TILE = 256
+ROWS = 32
 
 
 def remote(src, dst, send, recv, **where):
@@ -24,18 +26,11 @@
     )
 
 
-def lane_tiles(v):
-    total = v[:, :LANES]
-    for i in range(1, v.shape[1] // LANES):
-        total = total + v[:, i * LANES:(i + 1) * LANES]
-    return total
-
-
 def inverse_factor(gram):
     r, width = gram.shape
     row = lax.broadcasted_iota(jnp.int32, (r, width), 0)
     lane = lax.broadcasted_iota(jnp.int32, (r, width), 1)
-    work = jnp.where(lane == row + r, 1.0, gram)
+    work = jnp.where(lane < r, gram, jnp.where(lane == row + r, 1.0, 0.0))
     done = []
     for j0 in range(0, r, 4):
         base = (j0 // 8) * 8
@@ -44,7 +39,10 @@
         cols = [jnp.broadcast_to(work[:, j0 + k:j0 + k + 1], work.shape) for k in range(4)]
         rows = [work[o + k:o + k + 1, :] for k in range(4)]
         for k in range(4):
-            scale = 1.0 / cols[k][o + k:o + k + 1, :]
+            pivot = cols[k][o + k:o + k + 1, :]
+            scale = pl.reciprocal(pivot, approx=True)
+            scale = scale * (2.0 - pivot * scale)
+            scale = scale * (2.0 - pivot * scale)
             for m in range(k + 1, 4):
                 f = cols[m][o + k:o + k + 1, :] * scale
                 rows[m] = rows[m] - f * rows[k]
@@ -62,7 +60,7 @@
     n, sections, tokens_all,
     x_hbm, gain_hbm, left_hbm, r_hbm, b_hbm,
     gain_out, bias_out, left_out, right_out,
-    gain_ref, left_ref, x_v, rt, bt, scaled_v, bnd, acc1, acc2, terms, terms_in, grams, ortho_v,
+    gain_ref, left_ref, x_v, rt, bt, scaled_v, bnd, acc1, acc2, wide, terms, terms_in, grams, ortho_v,
     sib_out, sib_in, cross_out, cross_in, shift_v,
     local_sem, r_recv, r_cross, r_sib, r_fwd, b_recv, b_cross, b_sib, b_fwd,
     t_send, t_recv, g_send, g_recv, o_send, o_recv,
@@ -131,19 +129,31 @@
             to_cross(r_hbm, rt, r_recv, r_cross, o, p).start()
     for p in range(IN_PIECES):
         to_sib(r_hbm, rt, r_recv, r_sib, p).start()
+    for p in range(IN_PIECES):
+        for o in range(1, chips):
+            to_cross(b_hbm, bt, b_recv, b_cross, o, p).start()
 
     step = d // 12
     loads[1].wait()
 
+    def tiles(i):
+        for c in range(step // LANES):
+            yield x_v[:, pl.ds(pl.multiple_of(i * step + c * LANES, LANES), LANES)].astype(F32)
+
     def sum_step(i, acc):
-        return acc + lane_tiles(x_v[:, pl.ds(pl.multiple_of(i * step, LANES), step)].astype(F32))
+        for tile in tiles(i):
+            acc = acc + tile
+        return acc
 
     zero = jnp.zeros((tokens, LANES), F32)
     mu = jnp.sum(lax.fori_loop(0, 12, sum_step, zero), axis=1, keepdims=True) / d
+    mu_wide = jnp.broadcast_to(mu, (tokens, LANES))
 
     def square_step(i, acc):
-        c = x_v[:, pl.ds(pl.multiple_of(i * step, LANES), step)].astype(F32) - mu
-        return acc + lane_tiles(c * c)
+        for tile in tiles(i):
+            c = tile - mu_wide
+            acc = acc + c * c
+        return acc
 
     var = jnp.sum(lax.fori_loop(0, 12, square_step, zero), axis=1, keepdims=True) / d
     inverse = lax.rsqrt(var + 1e-5)
@@ -152,19 +162,35 @@
     left = left_ref[...].astype(F32).T.astype(BF16)
     acc1[...] = zero
     acc2[...] = zero
+    wide[0] = mu_wide
+    wide[1] = jnp.broadcast_to(inverse, (tokens, LANES))
 
     def first_pass(j, p):
-        at = columns(j, p)
-        rebuilt = lax.dot_general(left, rt[j, :, piece(p)], NN, preferred_element_type=F32)
-        normed = (x_v[:, at].astype(F32) - mu) * inverse
-        product = rebuilt * normed
-        terms[j, 0:1, piece(p)] = jnp.sum(product, axis=0, keepdims=True)
-        terms[j, 1:2, piece(p)] = jnp.sum(rebuilt, axis=0, keepdims=True)
-        gain = gain_ref[:, at]
-        scaled = rebuilt * gain
-        scaled_v[:, at] = scaled
-        acc1[...] += lane_tiles(scaled)
-        acc2[...] += lane_tiles(product * gain)
+        for c in range(pw // TILE):
+            inside = pl.ds(pl.multiple_of(p * pw + c * TILE, LANES), TILE)
+            rebuilt_tile = lax.dot_general(left, rt[j, :, inside], NN, preferred_element_type=F32)
+            for l in range(TILE // LANES):
+                offset = p * pw + c * TILE + l * LANES
+                local = pl.ds(pl.multiple_of(offset, LANES), LANES)
+                at = pl.ds(pl.multiple_of(j * w + offset, LANES), LANES)
+                gain = jnp.broadcast_to(gain_ref[:, at], (8, LANES))[None]
+                gain_sum = jnp.zeros((8, LANES), F32)
+                bias_sum = jnp.zeros((8, LANES), F32)
+                for h in range(0, tokens, ROWS):
+                    rows = pl.ds(h, ROWS)
+                    shape = (ROWS // 8, 8, LANES)
+                    rebuilt = rebuilt_tile[h:h + ROWS, l * LANES:(l + 1) * LANES]
+                    normed = (x_v[rows, at].astype(F32) - wide[0, rows, :]) * wide[1, rows, :]
+                    product = (rebuilt * normed).reshape(shape)
+                    rebuilt = rebuilt.reshape(shape)
+                    gain_sum = gain_sum + jnp.sum(product, axis=0)
+                    bias_sum = bias_sum + jnp.sum(rebuilt, axis=0)
+                    scaled = (rebuilt * gain).reshape(ROWS, LANES)
+                    scaled_v[rows, at] = scaled
+                    acc1[rows, :] += scaled
+                    acc2[rows, :] += (product * gain).reshape(ROWS, LANES)
+                terms[j, 0:1, local] = jnp.sum(gain_sum, axis=0, keepdims=True)
+                terms[j, 1:2, local] = jnp.sum(bias_sum, axis=0, keepdims=True)
 
     def loop(count, body):
         lax.fori_loop(0, count, lambda i, _: (body(i), 0)[1], 0)
@@ -183,7 +209,6 @@
         p, o = i // (chips - 1), 1 + i % (chips - 1)
         arrived(rt, r_recv, r_sib, source(o), p)
         forward(rt, r_recv, r_fwd, o, p).start()
-        to_cross(b_hbm, bt, b_recv, b_cross, o, p).start()
         first_pass(source(o), p)
 
     loop(IN_PIECES * (chips - 1), cross_first)
@@ -199,10 +224,16 @@
     m1 = jnp.sum(acc1[...], axis=1, keepdims=True) / d * inverse
     m2 = jnp.sum(acc2[...], axis=1, keepdims=True) / d * inverse * inverse
 
+    wide[0] = jnp.broadcast_to(m1 - mu * m2, (tokens, LANES))
+    wide[2] = jnp.broadcast_to(m2, (tokens, LANES))
+
     def second_pass(j, p):
-        at = columns(j, p)
-        center = x_v[:, at].astype(F32) - mu
-        bnd[:, at] = (scaled_v[:, at] * inverse - m1 - center * m2).astype(BF16)
+        for h in range(0, tokens, ROWS):
+            rows = pl.ds(h, ROWS)
+            shift, scale, slope = wide[0, rows, :], wide[1, rows, :], wide[2, rows, :]
+            for l in range(pw // LANES):
+                at = pl.ds(pl.multiple_of(j * w + p * pw + l * LANES, LANES), LANES)
+                bnd[rows, at] = (scaled_v[rows, at] * scale - x_v[rows, at].astype(F32) * slope - shift).astype(BF16)
 
     def project(j, p):
         acc1[0:64, :] += lax.dot_general(bt[j, :, piece(p)], bnd[:, columns(j, p)], NT, preferred_element_type=F32)
@@ -242,8 +273,12 @@
 
     r = left_ref.shape[0]
     power = acc1[0:64, :]
+    half = r // 2
     tall = jnp.concatenate([power, jnp.zeros_like(power)], axis=0)
-    grams[me] = lax.dot_general(power, tall, NT, precision=HIGH, preferred_element_type=F32)
+    low = jnp.concatenate([jnp.zeros_like(power), power], axis=0)
+    grams[me] = lax.dot_general(
+        power[0:half], tall, NT, precision=HIGH, preferred_element_type=F32
+    ) + lax.dot_general(power[half:r], low, NT, precision=HIGH, preferred_element_type=F32)
 
     def gram_copy(i):
         return remote(grams.at[me], grams.at[me], g_send.at[i], g_recv.at[me], dp=(me + i) % n)
@@ -255,15 +290,14 @@
     for i in range(1, n):
         gram_copy(i).start()
     for i in range(1, n):
-        terms_copy(i).start()
-    for i in range(1, n):
         j = (me + i) % n
         remote(grams.at[j], grams.at[j], g_send.at[0], g_recv.at[j], dp=sib).wait_recv()
-    gram = grams[0]
+    for i in range(1, n):
+        terms_copy(i).start()
+    packed = grams[0]
     for j in range(1, n):
-        gram = gram + grams[j]
-    factor = inverse_factor(gram)
-    low = jnp.concatenate([jnp.zeros_like(power), power], axis=0)
+        packed = packed + grams[j]
+    factor = inverse_factor(jnp.concatenate([packed, pltpu.roll(packed, r, 1)], axis=0))
     ortho = lax.dot_general(factor, low, NN, precision=HIGH, preferred_element_type=F32).astype(BF16)
     ortho_v[...] = ortho
 
@@ -381,10 +415,14 @@
 
 
 def write_out(*refs):
-    copies = [pltpu.make_async_copy(refs[i], refs[4 + i], refs[8].at[i]) for i in range(4)]
-    for copy in copies:
+    come = [pltpu.make_async_copy(refs[i], refs[8 + i], refs[12].at[i]) for i in range(4)]
+    go = [pltpu.make_async_copy(refs[8 + i], refs[4 + i], refs[13].at[i]) for i in range(4)]
+    for copy in come:
         copy.start()
-    for copy in copies:
+    for first, second in zip(come, go):
+        first.wait()
+        second.start()
+    for copy in go:
         copy.wait()
 
 
@@ -418,9 +456,10 @@
             pltpu.VMEM((tokens, d), BF16),
             pltpu.VMEM((tokens, LANES), F32),
             pltpu.VMEM((tokens, LANES), F32),
+            pltpu.VMEM((3, tokens, LANES), F32),
             pltpu.VMEM((n, 2, w), F32),
             pltpu.VMEM((n, 2, w), F32),
-            pltpu.VMEM((n, r, 2 * r), F32),
+            pltpu.VMEM((n, r // 2, 2 * r), F32),
             pltpu.VMEM((r, tokens), BF16),
             pltpu.VMEM((chips, r, w), BF16),
             pltpu.VMEM((chips, r, w), BF16),
@@ -446,7 +485,7 @@
         out_shape=results,
         in_specs=[hbm] * 4,
         out_specs=(hbm,) * 4,
-        scratch_shapes=[dma((4,))],
+        scratch_shapes=[*(pltpu.VMEM(a.shape, a.dtype) for a in results), dma((4,)), dma((4,))],
         compiler_params=pltpu.CompilerParams(vmem_limit_bytes=63 * 1024 * 1024),
     )(*held)
     return gain, bias, left.T[None], right.T[None]

time: 61.5 us -> 49.2 us (0.80)
  Pallas kernels: 60.7 us -> 48.3 us
    pallas_call x1, Pallas kernels: 14.3 us -> 1.86 us  [on_device(): pl.pallas_call(write_out, out_shape=results, in_specs=[hbm] * 4, out_spec...]
where the time goes in v4:
time: 49.2 us; the launch traced here: 48.9 us
  Pallas kernels  48.3 us (98%)
  between operations  0.64 us (1%)
    pallas_call x1, Pallas kernels, on_device(): pl.pallas_call(functools.partial(kernel, n, sections, tokens * n), out_sh...  46.4 us
    pallas_call x1, Pallas kernels, on_device(): pl.pallas_call(write_out, out_shape=results, in_specs=[hbm] * 4, out_spec...  1.86 us

profile of v4, /device:TPU:0, one launch (start us, length us, event | category | flops | bytes accessed | tf_op | source)
XLA Modules:
  0.0 48.9 jit_solution(11439454995516746215)
XLA Ops:
  0.6 46.4 %shard_map.84 = (f32[1,3072]{1,0:T(1,128)}, f32[1,3072]{1,0:T(1,128)}, bf16[64,128]{1,0:T(8,128)(2,1)}, bf16[64,3072]{1,0:T(8,128)(2,1)}) custom-call(bf16[128,12288]{1,0:T(8,128)(2,1)} %bitcast.16, f32[1,12288]{1,0:T(1,128)} %gain_hbm.1, bf16[64,128]{1,0:T(8,128)(2,1)} %bitcast.19, bf16[64,3072]{1,0:T(8,128)(2,1)} %bitcast.17, bf16[64,3072]{1,0:T(8,128)(2,1)} %bitcast.18), custom_call_target="tpu_custom_call" | custom-call | tf_op jit(solution)/shard_map/pallas_call | solution.py:444
  47.1 1.9 %shard_map.85 = (f32[1,3072]{1,0:T(1,128)}, f32[1,3072]{1,0:T(1,128)}, bf16[64,128]{1,0:T(8,128)(2,1)}, bf16[64,3072]{1,0:T(8,128)(2,1)}) custom-call(f32[1,3072]{1,0:T(1,128)} %get-tuple-element.12.refs_0_, f32[1,3072]{1,0:T(1,128)} %get-tuple-element.13.refs_1_, bf16[64,128]{1,0:T(8,128)(2,1)} %get-tuple-element.14.refs_2_, ...), custom_call_target="tpu_custom_call" | custom-call | tf_op jit(solution)/shard_map/pallas_call | solution.py:483

commit v5 on v3

--- a/solution.py
+++ b/solution.py
@@ -15,6 +15,8 @@
 LANES = 128
 IN_PIECES = 3
 OUT_PIECES = 6
+TILE = 256
+ROWS = 32
 
 
 def remote(src, dst, send, recv, **where):
@@ -22,13 +24,6 @@
         src_ref=src, dst_ref=dst, send_sem=send, recv_sem=recv,
         device_id=where, device_id_type=pl.DeviceIdType.MESH,
     )
-
-
-def lane_tiles(v):
-    total = v[:, :LANES]
-    for i in range(1, v.shape[1] // LANES):
-        total = total + v[:, i * LANES:(i + 1) * LANES]
-    return total
 
 
 def inverse_factor(gram):
@@ -44,7 +39,10 @@
         cols = [jnp.broadcast_to(work[:, j0 + k:j0 + k + 1], work.shape) for k in range(4)]
         rows = [work[o + k:o + k + 1, :] for k in range(4)]
         for k in range(4):
-            scale = 1.0 / cols[k][o + k:o + k + 1, :]
+            pivot = cols[k][o + k:o + k + 1, :]
+            scale = pl.reciprocal(pivot, approx=True)
+            scale = scale * (2.0 - pivot * scale)
+            scale = scale * (2.0 - pivot * scale)
             for m in range(k + 1, 4):
                 f = cols[m][o + k:o + k + 1, :] * scale
                 rows[m] = rows[m] - f * rows[k]
@@ -62,7 +60,7 @@
     n, sections, tokens_all,
     x_hbm, gain_hbm, left_hbm, r_hbm, b_hbm,
     gain_out, bias_out, left_out, right_out,
-    gain_ref, left_ref, x_v, rt, bt, scaled_v, bnd, acc1, acc2, terms, terms_in, grams, ortho_v, power_v, pre, conditioner,
+    gain_ref, left_ref, x_v, rt, bt, scaled_v, bnd, acc1, acc2, wide, terms, terms_in, grams, ortho_v, power_v, pre, conditioner,
     sib_out, sib_in, cross_out, cross_in, shift_v,
     local_sem, r_recv, r_cross, r_sib, r_fwd, b_recv, b_cross, b_sib, b_fwd,
     p_send, p_recv, t_send, t_recv, g_send, g_recv, o_send, o_recv,
@@ -131,19 +129,27 @@
             to_cross(r_hbm, rt, r_recv, r_cross, o, p).start()
     for p in range(IN_PIECES):
         to_sib(r_hbm, rt, r_recv, r_sib, p).start()
-
     step = d // 12
     loads[1].wait()
 
+    def tiles(i):
+        for c in range(step // LANES):
+            yield x_v[:, pl.ds(pl.multiple_of(i * step + c * LANES, LANES), LANES)].astype(F32)
+
     def sum_step(i, acc):
-        return acc + lane_tiles(x_v[:, pl.ds(pl.multiple_of(i * step, LANES), step)].astype(F32))
+        for tile in tiles(i):
+            acc = acc + tile
+        return acc
 
     zero = jnp.zeros((tokens, LANES), F32)
     mu = jnp.sum(lax.fori_loop(0, 12, sum_step, zero), axis=1, keepdims=True) / d
+    mu_wide = jnp.broadcast_to(mu, (tokens, LANES))
 
     def square_step(i, acc):
-        c = x_v[:, pl.ds(pl.multiple_of(i * step, LANES), step)].astype(F32) - mu
-        return acc + lane_tiles(c * c)
+        for tile in tiles(i):
+            c = tile - mu_wide
+            acc = acc + c * c
+        return acc
 
     var = jnp.sum(lax.fori_loop(0, 12, square_step, zero), axis=1, keepdims=True) / d
     inverse = lax.rsqrt(var + 1e-5)
@@ -152,6 +158,8 @@
     left = left_ref[...].astype(F32).T.astype(BF16)
     acc1[...] = zero
     acc2[...] = zero
+    wide[0] = mu_wide
+    wide[1] = jnp.broadcast_to(inverse, (tokens, LANES))
 
     loads[0].wait()
     loads[2].wait()
@@ -187,18 +195,36 @@
     for i in range(1, n):
         pre_copy(i).start()
 
+    for p in range(IN_PIECES):
+        for o in range(1, chips):
+            to_cross(b_hbm, bt, b_recv, b_cross, o, p).start()
+
     def first_pass(j, p):
-        at = columns(j, p)
-        rebuilt = lax.dot_general(left, rt[j, :, piece(p)], NN, preferred_element_type=F32)
-        normed = (x_v[:, at].astype(F32) - mu) * inverse
-        product = rebuilt * normed
-        terms[j, 0:1, piece(p)] = jnp.sum(product, axis=0, keepdims=True)
-        terms[j, 1:2, piece(p)] = jnp.sum(rebuilt, axis=0, keepdims=True)
-        gain = gain_ref[:, at]
-        scaled = rebuilt * gain
-        scaled_v[:, at] = scaled
-        acc1[...] += lane_tiles(scaled)
-        acc2[...] += lane_tiles(product * gain)
+        for c in range(pw // TILE):
+            inside = pl.ds(pl.multiple_of(p * pw + c * TILE, LANES), TILE)
+            rebuilt_tile = lax.dot_general(left, rt[j, :, inside], NN, preferred_element_type=F32)
+            for l in range(TILE // LANES):
+                offset = p * pw + c * TILE + l * LANES
+                local = pl.ds(pl.multiple_of(offset, LANES), LANES)
+                at = pl.ds(pl.multiple_of(j * w + offset, LANES), LANES)
+                gain = jnp.broadcast_to(gain_ref[:, at], (8, LANES))[None]
+                gain_sum = jnp.zeros((8, LANES), F32)
+                bias_sum = jnp.zeros((8, LANES), F32)
+                for h in range(0, tokens, ROWS):
+                    rows = pl.ds(h, ROWS)
+                    shape = (ROWS // 8, 8, LANES)
+                    rebuilt = rebuilt_tile[h:h + ROWS, l * LANES:(l + 1) * LANES]
+                    normed = (x_v[rows, at].astype(F32) - wide[0, rows, :]) * wide[1, rows, :]
+                    product = (rebuilt * normed).reshape(shape)
+                    rebuilt = rebuilt.reshape(shape)
+                    gain_sum = gain_sum + jnp.sum(product, axis=0)
+                    bias_sum = bias_sum + jnp.sum(rebuilt, axis=0)
+                    scaled = (rebuilt * gain).reshape(ROWS, LANES)
+                    scaled_v[rows, at] = scaled
+                    acc1[rows, :] += scaled
+                    acc2[rows, :] += (product * gain).reshape(ROWS, LANES)
+                terms[j, 0:1, local] = jnp.sum(gain_sum, axis=0, keepdims=True)
+                terms[j, 1:2, local] = jnp.sum(bias_sum, axis=0, keepdims=True)
 
     def loop(count, body):
         lax.fori_loop(0, count, lambda i, _: (body(i), 0)[1], 0)
@@ -215,7 +241,6 @@
         p, o = i // (chips - 1), 1 + i % (chips - 1)
         arrived(rt, r_recv, r_sib, source(o), p)
         forward(rt, r_recv, r_fwd, o, p).start()
-        to_cross(b_hbm, bt, b_recv, b_cross, o, p).start()
         first_pass(source(o), p)
 
     loop(IN_PIECES * (chips - 1), cross_first)
@@ -251,10 +276,16 @@
     m1 = jnp.sum(acc1[...], axis=1, keepdims=True) / d * inverse
     m2 = jnp.sum(acc2[...], axis=1, keepdims=True) / d * inverse * inverse
 
+    wide[0] = jnp.broadcast_to(m1 - mu * m2, (tokens, LANES))
+    wide[2] = jnp.broadcast_to(m2, (tokens, LANES))
+
     def second_pass(j, p):
-        at = columns(j, p)
-        center = x_v[:, at].astype(F32) - mu
-        bnd[:, at] = (scaled_v[:, at] * inverse - m1 - center * m2).astype(BF16)
+        for h in range(0, tokens, ROWS):
+            rows = pl.ds(h, ROWS)
+            shift, scale, slope = wide[0, rows, :], wide[1, rows, :], wide[2, rows, :]
+            for l in range(pw // LANES):
+                at = pl.ds(pl.multiple_of(j * w + p * pw + l * LANES, LANES), LANES)
+                bnd[rows, at] = (scaled_v[rows, at] * scale - x_v[rows, at].astype(F32) * slope - shift).astype(BF16)
 
     def project(j, p):
         acc1[0:r, :] += lax.dot_general(bt[j, :, piece(p)], bnd[:, columns(j, p)], NT, preferred_element_type=F32)
@@ -339,6 +370,7 @@
 
     for i in range(1, n):
         gram_copy(i).start()
+
 
     def stage_b(i):
         o, q = split(i)
@@ -480,6 +512,7 @@
             pltpu.VMEM((tokens, d), BF16),
             pltpu.VMEM((tokens, LANES), F32),
             pltpu.VMEM((tokens, LANES), F32),
+            pltpu.VMEM((3, tokens, LANES), F32),
             pltpu.VMEM((n, 2, w), F32),
             pltpu.VMEM((n, 2, w), F32),
             pltpu.VMEM((n, r // 2, 2 * r), F32),

time: 54.4 us -> 54.5 us (level)
  no operation moved by 1% of the time
where the time goes in v5:
time: 54.5 us; the launch traced here: 54.3 us
  Pallas kernels  53.7 us (99%)
  between operations  0.64 us (1%)
    pallas_call x1, Pallas kernels, on_device(): pl.pallas_call(functools.partial(kernel, n, sections, tokens * n), out_sh...  51.8 us
    pallas_call x1, Pallas kernels, on_device(): pl.pallas_call(write_out, out_shape=results, in_specs=[hbm] * 4, out_spec...  1.86 us

profile of v5, /device:TPU:0, one launch (start us, length us, event | category | flops | bytes accessed | tf_op | source)
XLA Modules:
  0.0 54.3 jit_solution(291415155766377587)
XLA Ops:
  0.6 51.8 %shard_map.84 = (f32[1,3072]{1,0:T(1,128)}, f32[1,3072]{1,0:T(1,128)}, bf16[64,128]{1,0:T(8,128)(2,1)}, bf16[64,3072]{1,0:T(8,128)(2,1)}) custom-call(bf16[128,12288]{1,0:T(8,128)(2,1)} %bitcast.16, f32[1,12288]{1,0:T(1,128)} %gain_hbm.1, bf16[64,128]{1,0:T(8,128)(2,1)} %bitcast.19, bf16[64,3072]{1,0:T(8,128)(2,1)} %bitcast.17, bf16[64,3072]{1,0:T(8,128)(2,1)} %bitcast.18), custom_call_target="tpu_custom_call" | custom-call | tf_op jit(solution)/shard_map/pallas_call | solution.py:500
  52.4 1.9 %shard_map.85 = (f32[1,3072]{1,0:T(1,128)}, f32[1,3072]{1,0:T(1,128)}, bf16[64,128]{1,0:T(8,128)(2,1)}, bf16[64,3072]{1,0:T(8,128)(2,1)}) custom-call(f32[1,3072]{1,0:T(1,128)} %get-tuple-element.12.refs_0_, f32[1,3072]{1,0:T(1,128)} %get-tuple-element.13.refs_1_, bf16[64,128]{1,0:T(8,128)(2,1)} %get-tuple-element.14.refs_2_, ...), custom_call_target="tpu_custom_call" | custom-call | tf_op jit(solution)/shard_map/pallas_call | solution.py:543

commit v6 on v4

--- a/solution.py
+++ b/solution.py
@@ -32,25 +32,22 @@
     lane = lax.broadcasted_iota(jnp.int32, (r, width), 1)
     work = jnp.where(lane < r, gram, jnp.where(lane == row + r, 1.0, 0.0))
     done = []
-    for j0 in range(0, r, 4):
-        base = (j0 // 8) * 8
-        o = j0 - base
-        rows_here = lax.broadcasted_iota(jnp.int32, work.shape, 0)
-        cols = [jnp.broadcast_to(work[:, j0 + k:j0 + k + 1], work.shape) for k in range(4)]
-        rows = [work[o + k:o + k + 1, :] for k in range(4)]
-        for k in range(4):
-            pivot = cols[k][o + k:o + k + 1, :]
+    for j0 in range(0, r, 8):
+        cols = [jnp.broadcast_to(work[:, j0 + k:j0 + k + 1], work.shape) for k in range(8)]
+        rows = [work[k:k + 1, :] for k in range(8)]
+        work = work[8:]
+        for k in range(8):
+            pivot = cols[k][k:k + 1, :]
             scale = pl.reciprocal(pivot, approx=True)
             scale = scale * (2.0 - pivot * scale)
             scale = scale * (2.0 - pivot * scale)
-            for m in range(k + 1, 4):
-                f = cols[m][o + k:o + k + 1, :] * scale
+            for m in range(k + 1, 8):
+                f = cols[m][k:k + 1, :] * scale
                 rows[m] = rows[m] - f * rows[k]
                 cols[m] = cols[m] - cols[k] * f
-            work = work - jnp.where(rows_here > o + k, cols[k], 0.0) * (rows[k] * scale)
-        if o == 4:
-            done.append(work[:8])
-            work = work[8:]
+            if j0 + 8 < r:
+                work = work - cols[k][8:] * (rows[k] * scale)
+        done.append(jnp.concatenate(rows, axis=0))
     full = jnp.concatenate(done, axis=0)
     diagonal = jnp.sum(jnp.where(lane == row, full, 0.0), axis=1, keepdims=True)
     return full * lax.rsqrt(diagonal)

time: 49.2 us -> 48.5 us (0.986)
  Pallas kernels: 48.3 us -> 47.7 us
    pallas_call x1, Pallas kernels: 46.4 us -> 45.8 us  [on_device(): pl.pallas_call(functools.partial(kernel, n, sections, tokens * n), out_sh...]
where the time goes in v6:
time: 48.5 us; the launch traced here: 48.3 us
  Pallas kernels  47.7 us (98%)
  between operations  0.64 us (1%)
    pallas_call x1, Pallas kernels, on_device(): pl.pallas_call(functools.partial(kernel, n, sections, tokens * n), out_sh...  45.8 us
    pallas_call x1, Pallas kernels, on_device(): pl.pallas_call(write_out, out_shape=results, in_specs=[hbm] * 4, out_spec...  1.86 us

profile of v6, /device:TPU:0, one launch (start us, length us, event | category | flops | bytes accessed | tf_op | source)
XLA Modules:
  0.0 48.3 jit_solution(483784134986326299)
XLA Ops:
  0.6 45.8 %shard_map.84 = (f32[1,3072]{1,0:T(1,128)}, f32[1,3072]{1,0:T(1,128)}, bf16[64,128]{1,0:T(8,128)(2,1)}, bf16[64,3072]{1,0:T(8,128)(2,1)}) custom-call(bf16[128,12288]{1,0:T(8,128)(2,1)} %bitcast.16, f32[1,12288]{1,0:T(1,128)} %gain_hbm.1, bf16[64,128]{1,0:T(8,128)(2,1)} %bitcast.19, bf16[64,3072]{1,0:T(8,128)(2,1)} %bitcast.17, bf16[64,3072]{1,0:T(8,128)(2,1)} %bitcast.18), custom_call_target="tpu_custom_call" | custom-call | tf_op jit(solution)/shard_map/pallas_call | solution.py:441
  46.4 1.9 %shard_map.85 = (f32[1,3072]{1,0:T(1,128)}, f32[1,3072]{1,0:T(1,128)}, bf16[64,128]{1,0:T(8,128)(2,1)}, bf16[64,3072]{1,0:T(8,128)(2,1)}) custom-call(f32[1,3072]{1,0:T(1,128)} %get-tuple-element.12.refs_0_, f32[1,3072]{1,0:T(1,128)} %get-tuple-element.13.refs_1_, bf16[64,128]{1,0:T(8,128)(2,1)} %get-tuple-element.14.refs_2_, ...), custom_call_target="tpu_custom_call" | custom-call | tf_op jit(solution)/shard_map/pallas_call | solution.py:480
